TPU v7x, 128 devices: a whole 4x4x4 slice. The times are simulated.
128 devices in a mesh: dp: 2 (over core), expert: 64 (over z, y, x).
Axes of the slice: x: 4, y: 4, z: 4, core: 2. Of those that a mesh axis runs over, the one named last changes fastest.
Arguments:
- tokens: bfloat16 [32768, 3584], P(('dp', 'expert')), may hold values from -6 to 6
- expert_ids: int32 [32768, 2], P(('dp', 'expert')), may hold values from 0 to 63, all different within a row; in each aligned block of 256 rows (0 to 255, 256 to 511, ...) at most 12 rows name the same one
- gate_weights: float32 [32768, 2], P(('dp', 'expert')), may hold values from 0.2 to 1
- w_in: bfloat16 [64, 3584, 2560], P('expert', None, 'dp'), may hold values from -0.09375 to 0.09375
- w_out: bfloat16 [64, 2560, 3584], P('expert', 'dp'), may hold values from -0.125 to 0.125
Outputs:
- mixed: bfloat16 [32768, 3584], P(('dp', 'expert'))
Inputs may be any that keep to these rules, and one draw needn't show every extreme that they name: `expert_ids`: each row names 2 different experts. Among the rows of one device no expert is named more than 12 times, and in every draw some device names some expert exactly 12 times.
All inputs are finite; a program needn't handle non-finite values.
Results may differ from a plain program's by a relative error of at most 0.007.
Values may be sent and summed in bfloat16 or wider, within the bound.
No kernel may reach another device: no remote copies, remote signals or barrier semaphores. Data moves between devices by JAX's collectives and lax.ppermute only.
A program may use at most 192 MiB of HBM per device.

v0:
```python
import jax
import jax.numpy as jnp
from jax import lax
from jax.sharding import PartitionSpec as P


def per_device(tokens, expert_ids, gate_weights, w_in, w_out):
    local_rows, model_width = tokens.shape
    top_count = expert_ids.shape[1]
    peer_count = lax.axis_size("expert")
    shard_width = w_out.shape[1]
    capacity = max(2, 3 * local_rows * top_count // (2 * peer_count))
    flat_ids = expert_ids.reshape(-1)
    one_hot = (flat_ids[:, None] == jnp.arange(peer_count, dtype=jnp.int32)[None, :]).astype(
        jnp.int32
    )
    position = jnp.sum((jnp.cumsum(one_hot, 0) - 1) * one_hot, 1)
    target = flat_ids * capacity + position
    repeated = jnp.repeat(tokens, top_count, 0)
    send_buffer = (
        jnp.zeros((peer_count * capacity, model_width), tokens.dtype).at[target].set(repeated)
    )
    received = lax.all_to_all(
        send_buffer.reshape(peer_count, capacity, model_width),
        "expert",
        split_axis=0,
        concat_axis=0,
        tiled=True,
    )
    arrived = received.reshape(peer_count * capacity, model_width)
    hidden = jax.nn.silu(
        jnp.dot(
            arrived,
            lax.all_gather(w_in, "dp", axis=2, tiled=True)[0],
            preferred_element_type=jnp.float32,
        )
    ).astype(jnp.bfloat16)
    empty = jnp.zeros((arrived.shape[0], model_width), jnp.float32)
    running = empty
    shard_piece = lax.all_gather(w_out, "dp", axis=1, tiled=True)
    for block in range(shard_piece.shape[1] // shard_width):
        columns = lax.dynamic_slice_in_dim(hidden, block * shard_width, shard_width, 1)
        part_sum = jnp.dot(
            columns,
            shard_piece[0, block * shard_width : (block + 1) * shard_width],
            preferred_element_type=jnp.float32,
        )
        running = running + part_sum.astype(jnp.bfloat16).astype(jnp.float32)
    outgoing = running.astype(jnp.bfloat16).reshape(peer_count, capacity, model_width)
    returned = lax.all_to_all(outgoing, "expert", split_axis=0, concat_axis=0, tiled=True)
    picked = returned.reshape(peer_count * capacity, model_width)[target]
    picked = picked.astype(jnp.float32).reshape(local_rows, top_count, model_width)
    weighted = jnp.sum(gate_weights[:, :, None] * picked, 1)
    return (tokens.astype(jnp.float32) + weighted).astype(jnp.bfloat16)


def solution(mesh):
    placed = (
        P(("dp", "expert"), None),
        P(("dp", "expert"), None),
        P(("dp", "expert"), None),
        P("expert", None, "dp"),
        P("expert", "dp", None),
    )
    return jax.shard_map(
        per_device, mesh=mesh, in_specs=placed, out_specs=P(("dp", "expert"), None), check_vma=False
    )
```

profile of v0, /device:TPU:4, one launch (start us, length us, event | category | flops | bytes accessed | tf_op | source)
XLA Modules:
  0.0 387.0 jit_solution(12601159878032074085)
XLA Ops:
  6.5 0.7 all-gather.3.cloned.1.call-update
  7.3 0.7 all-gather.5.cloned.1.call-update
  8.2 0.1 eq.29
  8.5 1.2 reduce-window.6
  9.7 0.2 slice_reduce_fusion
  10.0 0.1 copy.8
  10.1 0.1 mul.34
  10.3 3.5 broadcast_in_dim.5
  13.8 8.5 %reshape.87 = bf16[512,3584]{1,0:T(8,128)(2,1)} reshape(bf16[256,2,3584]{2,1,0:T(2,128)(2,1)} %broadcast_in_dim.5) | data formatting | bytes 7340032 | tf_op jit(solution)/shard_map/reshape | solution.py:19
  22.4 11.7 %scatter_custom_fusion = bf16[768,3584]{1,0:T(8,128)(2,1)} fusion(s32[512]{0:T(512)S(1)} %bitcast.36, bf16[512,3584]{1,0:T(8,128)(2,1)} %reshape.87, bf16[]{:T(256)} %constant.7.clone.1), kind=kCustom, calls=%fused_computation.14 | custom fusion | bytes 5505536 | tf_op jit(solution)/shard_map/scatter | solution.py:21
  34.1 9.6 %reshape.70 = bf16[64,12,3584]{2,1,0:T(8,128)(2,1)} reshape(bf16[768,3584]{1,0:T(8,128)(2,1)} %scatter_custom_fusion) | data formatting | bytes 11010048 | tf_op jit(solution)/shard_map/reshape | solution.py:24
  43.7 96.1 %all_to_all.10 = bf16[64,12,3584]{2,1,0:T(8,128)(2,1)} all-to-all(bf16[64,12,3584]{2,1,0:T(8,128)(2,1)} %reshape.70), channel_id=1, replica_groups=mesh['dp'=2,'expert'=64] {'expert'}, dimensions={0} | all-to-all | bytes 11010048 | tf_op jit(solution)/shard_map/all_to_all | solution.py:23
  139.8 9.4 %reshape.71 = bf16[768,3584]{1,0:T(8,128)(2,1)} reshape(bf16[64,12,3584]{2,1,0:T(8,128)(2,1)} %all_to_all.10) | data formatting | bytes 11010048 | tf_op jit(solution)/shard_map/reshape | solution.py:30
  149.2 21.8 %multiply_convert_fusion = bf16[768,2560]{1,0:T(8,128)(2,1)} fusion(bf16[768,3584]{1,0:T(8,128)(2,1)} %reshape.71, bf16[1,3584,2560]{2,1,0:T(8,128)(2,1)} %all-gather.3.cloned.1.call-done), kind=kOutput, calls=%fused_computation.9 | convolution fusion | flops 14102691840 | bytes 27787264 | tf_op jit(solution)/shard_map/dot_general | solution.py:32
  171.0 12.1 %fusion.4 = bf16[768,3584]{1,0:T(8,128)(2,1)} fusion(bf16[1,2560,3584]{2,1,0:T(8,128)(2,1)} %all-gather.5.cloned.1.call-done, bf16[768,2560]{1,0:T(8,128)(2,1)} %multiply_convert_fusion), kind=kOutput, calls=%fused_computation.11 | convolution fusion | flops 7049183232 | bytes 16646144 | tf_op jit(solution)/shard_map/dot_general | solution.py:43
  183.1 11.4 %add_convert_fusion = bf16[768,3584]{1,0:T(8,128)(2,1)} fusion(bf16[768,3584]{1,0:T(8,128)(2,1)} %fusion.4, bf16[1,2560,3584]{2,1,0:T(8,128)(2,1)S(1)} %copy-done.3, bf16[768,2560]{1,0:T(8,128)(2,1)} %multiply_convert_fusion), kind=kOutput, calls=%fused_computation.4 | convolution fusion | flops 7060193280 | bytes 22151168 | tf_op jit(solution)/shard_map/dot_general | solution.py:43
  194.5 9.3 %reshape.72 = bf16[64,12,3584]{2,1,0:T(8,128)(2,1)} reshape(bf16[768,3584]{1,0:T(8,128)(2,1)} %add_convert_fusion) | data formatting | bytes 11010048 | tf_op jit(solution)/shard_map/reshape | solution.py:49
  203.8 7.7 %all-to-all-start.1 = ((bf16[64,12,3584]{2,1,0:T(8,128)(2,1)}), bf16[64,12,3584]{2,1,0:T(8,128)(2,1)}, u32[]{:S(2)}, u32[]{:S(2)}) async-start(bf16[64,12,3584]{2,1,0:T(8,128)(2,1)} %reshape.72), calls=%async_computation.1 | async-start | bytes 14680064 | tf_op jit(solution)/shard_map/all_to_all | solution.py:50
  211.7 102.3 %all-to-all-done.1 = bf16[64,12,3584]{2,1,0:T(8,128)(2,1)} async-done(((bf16[64,12,3584]{2,1,0:T(8,128)(2,1)}), bf16[64,12,3584]{2,1,0:T(8,128)(2,1)}, u32[]{:S(2)}, u32[]{:S(2)}) %all-to-all-start.1) | async-done | bytes 5505056 | tf_op jit(solution)/shard_map/all_to_all | solution.py:50
  314.0 9.4 %reshape.73 = bf16[768,3584]{1,0:T(8,128)(2,1)} reshape(bf16[64,12,3584]{2,1,0:T(8,128)(2,1)} %all-to-all-done.1) | data formatting | bytes 11010048 | tf_op jit(solution)/shard_map/reshape | solution.py:51
  323.4 11.2 %gather_fusion = bf16[512,3584]{1,0:T(8,128)(2,1)} fusion(bf16[768,3584]{1,0:T(8,128)(2,1)} %reshape.73, s32[1024]{0:T(1024)S(1)} %pad_clamp_fusion), kind=kCustom, calls=%fused_computation | custom fusion | bytes 7342080 | tf_op jit(solution)/shard_map/gather | solution.py:51
  334.6 8.6 %reshape.74 = f32[256,2,3584]{2,1,0:T(2,128)} reshape(bf16[512,3584]{1,0:T(8,128)(2,1)} %gather_fusion) | data formatting | bytes 11010048 | tf_op jit(solution)/shard_map/convert_element_type | solution.py:52
  343.2 35.3 %multiply_reduce_fusion = f32[256,3584]{1,0:T(8,128)S(1)} fusion(f32[256,2,3584]{2,1,0:T(2,128)} %reshape.74, f32[256,2]{1,0:T(8,128)S(1)} %copy.7), kind=kLoop, calls=%fused_computation.10 | loop fusion | flops 2752512 | bytes 11012096 | tf_op jit(solution)/shard_map/reduce_sum | solution.py:53
  378.5 1.6 add_convert_fusion.1
  (22 shorter events, 0.6 us)
Async XLA Ops:
  6.5 142.7 %all-gather.3.cloned.1.call-start = ((), (), s32[]{:S(2)}) async-start(), calls=%async_computation.2 | async-start | bytes 27525120 | tf_op jit(solution)/shard_map/all_gather | solution.py:34
  7.3 0.8 copy-start.1
  7.3 3.0 copy-start
  7.3 163.7 %all-gather.5.cloned.1.call-start = ((), (), s32[]{:S(2)}) async-start(), calls=%async_computation.3 | async-start | bytes 27525120 | tf_op jit(solution)/shard_map/all_gather | solution.py:40
  171.0 12.1 %copy-start.3 = (bf16[1,2560,3584]{2,1,0:T(8,128)(2,1)S(1)}, bf16[1,2560,3584]{2,1,0:T(8,128)(2,1)}, u32[]{:S(2)}) copy-start(bf16[1,2560,3584]{2,1,0:T(8,128)(2,1)} %all-gather.5.cloned.1.call-done) | copy-start | bytes 55050244
  203.8 7.7 %copy-start.2 = (f32[256,2]{0,1:T(2,128)S(1)}, f32[256,2]{0,1:T(2,128)}, u32[]{:S(2)}) copy-start(f32[256,2]{0,1:T(2,128)} %param.7) | copy-start | bytes 6148
  203.8 110.2 %all-to-all-start.1 = ((bf16[64,12,3584]{2,1,0:T(8,128)(2,1)}), bf16[64,12,3584]{2,1,0:T(8,128)(2,1)}, u32[]{:S(2)}, u32[]{:S(2)}) async-start(bf16[64,12,3584]{2,1,0:T(8,128)(2,1)} %reshape.72), calls=%async_computation.1 | async-start | bytes 14680064 | tf_op jit(solution)/shard_map/all_to_all | solution.py:50
Sparse Core Ops, SparseCore 0:
  9.0 38.3 all-gather.2
  49.1 37.3 all-gather.4
where the time goes:
time: 389 us; the launch traced here: 387 us
  waiting for transfers between devices  104 us (27%)
  blocking collectives  96.1 us (25%)
  local copies, waits for them, and re-layouts  82.2 us (21%)
  matrix products  45.3 us (12%)
  other arithmetic  38.3 us (10%)
  between operations  13.5 us (3%)
  starting transfers between devices  7.77 us (2%)
    all_to_all x1, waiting for transfers between devices, per_device(): lax.all_to_all(outgoing, 'expert', split_axis=0, concat_axis=0, tiled=True)  102 us
    all_to_all x1, blocking collectives, per_device(): lax.all_to_all(send_buffer.reshape(peer_count, capacity, model_width), 'e...  96.1 us
    reduce_sum x1, other arithmetic, per_device(): weighted = jnp.sum(gate_weights[:, :, None] * picked, 1)  35.3 us
    dot_general x2, matrix products, per_device(): jnp.dot(columns, shard_piece[0, block * shard_width:(block + 1) * shard_w...  23.5 us
    dot_general x1, matrix products, per_device(): jnp.dot(arrived, lax.all_gather(w_in, 'dp', axis=2, tiled=True)[0], prefe...  21.8 us
    scatter x1, local copies, waits for them, and re-layouts, per_device(): jnp.zeros((peer_count * capacity, model_width), tokens.dtype).at[target]  11.7 us
    gather x1, local copies, waits for them, and re-layouts, per_device(): picked = returned.reshape(peer_count * capacity, model_width)[target]  11.2 us
    reshape x1, local copies, waits for them, and re-layouts, per_device(): send_buffer.reshape(peer_count, capacity, model_width)  9.62 us
  transfers between devices with their start and end apart: 3, of which 1 were waited for; matrix products, arithmetic and copies ran while one was open for 17% of the time, Pallas kernels for 0%

commit v1 on v0

v1 whole, which is shorter than its diff:
```python
import functools

import jax
import jax.numpy as jnp
from jax import lax
from jax.experimental import pallas as pl
from jax.experimental.pallas import tpu as pltpu
from jax.sharding import PartitionSpec as P

PACK = 8
EXTRA = 4
BF16 = jnp.bfloat16
F32 = jnp.float32


def iota(shape, dim):
    return lax.broadcasted_iota(jnp.int32, shape, dim)


def dot(a, b):
    return jnp.dot(a, b, preferred_element_type=F32)


def dot_t(a, b):
    return lax.dot_general(a, b, (((0,), (0,)), ((), ())), preferred_element_type=F32)


def prep_kernel(ids_ref, tok_ref, place_ref, out_ref, *, peers):
    tokens = tok_ref.shape[0]
    width = tok_ref.shape[1]
    half = width // 2
    rows = peers * PACK
    before = (iota((tokens, tokens), 0) < iota((tokens, tokens), 1)).astype(BF16)
    experts = iota((peers, tokens), 0)
    first = experts == ids_ref[0:1, :]
    second = experts == ids_ref[1:2, :]
    first_f, second_f = first.astype(F32), second.astype(F32)
    rank0 = jnp.sum(dot(first.astype(BF16), before) * first_f, 0, keepdims=True)
    count0 = jnp.sum(first_f, 1, keepdims=True)
    rank1 = jnp.sum((dot(second.astype(BF16), before) + count0) * second_f, 0, keepdims=True)
    rank = jnp.concatenate([rank0, rank1], 0).astype(jnp.int32)
    base = ids_ref[...] * PACK + rank
    whole = jnp.where(rank < PACK, base, -rows)
    split = jnp.where(rank < PACK, -rows, base - PACK)
    place_ref[0:2, :] = whole
    place_ref[2:4, :] = split
    row = iota((rows, tokens), 0)
    pick = ((row == whole[0:1, :]) | (row == whole[1:2, :])).astype(BF16)
    left = ((row == split[0:1, :]) | (row == split[1:2, :])).astype(BF16)
    right = ((row == split[0:1, :] + EXTRA) | (row == split[1:2, :] + EXTRA)).astype(BF16)
    step = width // 7
    for c in range(0, width, step):
        out_ref[:, c : c + step] = dot(pick, tok_ref[:, c : c + step]).astype(BF16)
    step = half // 7
    for c in range(0, half, step):
        part = dot(left, tok_ref[:, c : c + step])
        part = part + dot(right, tok_ref[:, half + c : half + c + step])
        out_ref[:, width + c : width + c + step] = part.astype(BF16)


def prep(ids, tokens, peers):
    count, width = tokens.shape
    return pl.pallas_call(
        functools.partial(prep_kernel, peers=peers),
        out_shape=(
            jax.ShapeDtypeStruct((4, count), jnp.int32),
            jax.ShapeDtypeStruct((peers * PACK, width + width // 2), BF16),
        ),
        compiler_params=pltpu.CompilerParams(vmem_limit_bytes=40 * 2**20),
        name="dispatch_rows",
    )(ids, tokens)


def combine_kernel(place_ref, gate_ref, tok_ref, back_ref, out_ref):
    tokens, width = tok_ref.shape
    half = width // 2
    rows = back_ref.shape[0]
    row = iota((rows, tokens), 0)
    g0, g1 = gate_ref[0:1, :], gate_ref[1:2, :]

    def weights(p0, p1):
        w = jnp.where(row == p0, g0, 0.0) + jnp.where(row == p1, g1, 0.0)
        high = w.astype(BF16)
        return high, (w - high.astype(F32)).astype(BF16)

    whole = weights(place_ref[0:1, :], place_ref[1:2, :])
    left = weights(place_ref[2:3, :], place_ref[3:4, :])
    right = weights(place_ref[2:3, :] + EXTRA, place_ref[3:4, :] + EXTRA)
    step = half // 7
    for side, extra in ((0, left), (1, right)):
        for c in range(0, half, step):
            at = side * half + c
            total = tok_ref[:, at : at + step].astype(F32)
            for w in whole:
                total = total + dot_t(w, back_ref[:, at : at + step])
            for w in extra:
                total = total + dot_t(w, back_ref[:, width + c : width + c + step])
            out_ref[:, at : at + step] = total.astype(BF16)


def combine(place, gates, tokens, back):
    return pl.pallas_call(
        combine_kernel,
        out_shape=jax.ShapeDtypeStruct(tokens.shape, BF16),
        compiler_params=pltpu.CompilerParams(vmem_limit_bytes=40 * 2**20),
        name="weighted_rows",
    )(place, gates, tokens, back)


def silu(v):
    return v / (1.0 + jnp.exp(-v))


def ffn_kernel(x_ref, win_ref, wout_ref, o_ref, x2, h, y2, *, n1, n2, fw, dw, mc):
    step = pl.program_id(0)
    rows = x_ref.shape[0]
    width = x2.shape[1]
    half = width // 2
    more = x2.shape[0]

    @pl.when(step == 0)
    def _():
        source = iota((more, rows), 0) // EXTRA * PACK + iota((more, rows), 0) % EXTRA
        column = iota((more, rows), 1)
        packed = x_ref[:, width:]
        x2[:, :half] = dot((source == column).astype(BF16), packed).astype(BF16)
        x2[:, half:] = dot((source + EXTRA == column).astype(BF16), packed).astype(BF16)

    @pl.when(step < n1)
    def _():
        c = pl.ds(pl.multiple_of(step * fw, fw), fw)
        for m in range(0, rows, mc):
            h[m : m + mc, c] = silu(dot(x_ref[m : m + mc, :width], win_ref[...])).astype(BF16)
        for m in range(0, more, mc):
            h[rows + m : rows + m + mc, c] = silu(dot(x2[m : m + mc, :], win_ref[...])).astype(BF16)

    @pl.when(step >= n1)
    def _():
        c = pl.ds(pl.multiple_of((step - n1) * dw, dw), dw)
        for m in range(0, rows, mc):
            o_ref[m : m + mc, c] = dot(h[m : m + mc, :], wout_ref[...]).astype(BF16)
        for m in range(0, more, mc):
            y2[m : m + mc, c] = dot(h[rows + m : rows + m + mc, :], wout_ref[...]).astype(BF16)

    @pl.when(step == n1 + n2 - 1)
    def _():
        row = iota((rows, more), 0)
        source = iota((rows, more), 1) // EXTRA * PACK + iota((rows, more), 1) % EXTRA
        packed = dot((row == source).astype(BF16), y2[:, :half])
        packed = packed + dot((row == source + EXTRA).astype(BF16), y2[:, half:])
        o_ref[:, width:] = packed.astype(BF16)


def ffn(x, w_in, w_out, fw=512, dw=512, mc=256):
    width, hidden = w_in.shape
    rows = x.shape[0]
    more = rows // PACK * EXTRA
    n1, n2 = hidden // fw, width // dw
    return pl.pallas_call(
        functools.partial(ffn_kernel, n1=n1, n2=n2, fw=fw, dw=dw, mc=mc),
        out_shape=jax.ShapeDtypeStruct(x.shape, BF16),
        grid=(n1 + n2,),
        in_specs=[
            pl.BlockSpec(x.shape, lambda i: (0, 0), pipeline_mode=pl.Buffered(1)),
            pl.BlockSpec((width, fw), lambda i: (0, jnp.minimum(i, n1 - 1))),
            pl.BlockSpec((hidden, dw), lambda i: (0, jnp.maximum(i - n1, 0))),
        ],
        out_specs=pl.BlockSpec(x.shape, lambda i: (0, 0), pipeline_mode=pl.Buffered(1)),
        scratch_shapes=[
            pltpu.VMEM((more, width), BF16),
            pltpu.VMEM((rows + more, hidden), BF16),
            pltpu.VMEM((more, width), BF16),
        ],
        compiler_params=pltpu.CompilerParams(vmem_limit_bytes=50 * 2**20),
        cost_estimate=pl.CostEstimate(
            flops=4 * (rows + more) * width * hidden,
            bytes_accessed=4 * width * hidden + 4 * x.size,
            transcendentals=(rows + more) * hidden,
        ),
        name="expert_layer",
    )(x, w_in, w_out)


def swap(x, peers):
    chunks = x.reshape(peers, x.shape[0] // peers, x.shape[1])
    return lax.all_to_all(chunks, "expert", split_axis=0, concat_axis=0, tiled=True).reshape(x.shape)


def per_device(tokens, expert_ids, gate_weights, w_in, w_out):
    peers = lax.axis_size("expert")
    full_in = lax.all_gather(w_in, "dp", axis=2, tiled=True)[0]
    full_out = lax.all_gather(w_out, "dp", axis=1, tiled=True)[0]
    place, sent = prep(expert_ids.T, tokens, peers)
    arrived = swap(sent, peers)
    outgoing = ffn(arrived, full_in, full_out)
    returned = swap(outgoing, peers)
    return combine(place, gate_weights.T, tokens, returned)


def solution(mesh):
    placed = (
        P(("dp", "expert"), None),
        P(("dp", "expert"), None),
        P(("dp", "expert"), None),
        P("expert", None, "dp"),
        P("expert", "dp", None),
    )
    return jax.shard_map(
        per_device, mesh=mesh, in_specs=placed, out_specs=P(("dp", "expert"), None), check_vma=False
    )
```

time: 389 us -> 217 us (0.56)
  the two profiles are of different devices: /device:TPU:4 before, /device:TPU:1 now
where the time goes in v1:
time: 217 us
  blocking collectives  153 us (71%)
  Pallas kernels  48.1 us (22%)
  between operations  13.4 us (6%)
    all_to_all x2, blocking collectives, swap(): lax.all_to_all(chunks, 'expert', split_axis=0, concat_axis=0, tiled=True)  153 us
    pallas_call x1, Pallas kernels, ffn(): pl.pallas_call(functools.partial(ffn_kernel, n1=n1, n2=n2, fw=fw, dw=dw,...  40.4 us
    pallas_call x1, Pallas kernels, combine(): pl.pallas_call(combine_kernel, out_shape=jax.ShapeDtypeStruct(tokens.shap...  5.46 us
  transfers between devices with their start and end apart: 2, of which 0 were waited for; matrix products, arithmetic and copies ran while one was open for 0% of the time, Pallas kernels for 1%

profile of v1, /device:TPU:1, one launch (start us, length us, event | category | flops | bytes accessed | tf_op | source)
XLA Modules:
  0.0 216.6 jit_solution(9714423089823944816)
XLA Ops:
  6.5 0.0 all-gather.3.cloned.1.call-start
  6.5 0.7 all-gather.3.cloned.1.call-update
  7.3 0.0 copy-start
  7.3 0.0 copy-start.2
  7.3 0.0 all-gather.5.cloned.1.call-start
  7.3 0.7 all-gather.5.cloned.1.call-update
  8.0 0.7 copy-done
  8.8 0.0 copy-done.2
  8.8 2.2 %dispatch_rows.1 = (s32[4,256]{1,0:T(4,128)S(1)}, bf16[512,5376]{1,0:T(8,128)(2,1)S(1)}) custom-call(s32[2,256]{1,0:T(2,128)S(1)} %bitcast.11, bf16[256,3584]{1,0:T(8,128)(2,1)S(1)} %copy-done), custom_call_target="tpu_custom_call" | custom-call | tf_op jit(solution)/shard_map/dispatch_rows/pallas_call | solution.py:63
  11.0 77.3 %all_to_all.10 = bf16[64,8,5376]{2,1,0:T(8,128)(2,1)} all-to-all(bf16[64,8,5376]{2,1,0:T(8,128)(2,1)S(1)} %bitcast.9), channel_id=1, replica_groups=mesh['dp'=2,'expert'=64] {'expert'}, dimensions={0} | all-to-all | bytes 11010048 | tf_op jit(solution)/shard_map/all_to_all | solution.py:186
  88.3 0.0 all-gather.3.cloned.1.call-done
  88.3 0.0 all-gather.5.cloned.1.call-done
  88.3 40.4 %expert_layer.1 = bf16[512,5376]{1,0:T(8,128)(2,1)} custom-call(bf16[512,5376]{1,0:T(8,128)(2,1)} %bitcast.12, bf16[3584,2560]{1,0:T(8,128)(2,1)} %bitcast.14, bf16[2560,3584]{1,0:T(8,128)(2,1)} %bitcast.15), custom_call_target="tpu_custom_call" | custom-call | flops 28185722880 | bytes 47710208 | tf_op jit(solution)/shard_map/expert_layer/pallas_call | solution.py:159
  128.7 0.0 copy-start.1
  128.7 75.6 %all_to_all.11 = bf16[64,8,5376]{2,1,0:T(8,128)(2,1)S(1)} all-to-all(bf16[64,8,5376]{2,1,0:T(8,128)(2,1)} %bitcast.13), channel_id=1, replica_groups=mesh['dp'=2,'expert'=64] {'expert'}, dimensions={0} | all-to-all | bytes 11010048 | tf_op jit(solution)/shard_map/all_to_all | solution.py:186
  204.3 0.0 copy-done.1
  204.3 5.5 %weighted_rows.1 = bf16[256,3584]{1,0:T(8,128)(2,1)} custom-call(s32[4,256]{1,0:T(4,128)S(1)} %get-tuple-element.7.place_ref, f32[2,256]{1,0:T(2,128)S(1)} %bitcast.10, bf16[256,3584]{1,0:T(8,128)(2,1)S(1)} %copy-done, bf16[512,5376]{1,0:T(8,128)(2,1)S(1)} %bitcast.8), custom_call_target="tpu_custom_call" | custom-call | tf_op jit(solution)/shard_map/weighted_rows/pallas_call | solution.py:102
Async XLA Ops:
  6.5 81.8 %all-gather.3.cloned.1.call-start = ((), (), s32[]{:S(2)}) async-start(), calls=%async_computation.2 | async-start | bytes 27525120 | tf_op jit(solution)/shard_map/all_gather | solution.py:191
  7.3 1.5 copy-start
  7.3 1.5 copy-start.2
  7.3 81.1 %all-gather.5.cloned.1.call-start = ((), (), s32[]{:S(2)}) async-start(), calls=%async_computation.3 | async-start | bytes 27525120 | tf_op jit(solution)/shard_map/all_gather | solution.py:192
  128.7 75.6 %copy-start.1 = (f32[256,2]{0,1:T(2,128)S(1)}, f32[256,2]{0,1:T(2,128)}, u32[]{:S(2)}) copy-start(f32[256,2]{0,1:T(2,128)} %param.7) | copy-start | bytes 6148
Sparse Core Ops, SparseCore 0:
  9.0 39.6 all-gather.2
  50.4 37.3 all-gather.4

commit v2 on v1

v2 whole, which is shorter than its diff:
```python
import functools

import jax
import jax.numpy as jnp
from jax import lax
from jax.experimental import pallas as pl
from jax.experimental.pallas import tpu as pltpu
from jax.sharding import PartitionSpec as P

PACK = 8
EXTRA = 4
BF16 = jnp.bfloat16
F32 = jnp.float32


def iota(shape, dim):
    return lax.broadcasted_iota(jnp.int32, shape, dim)


def dot(a, b):
    return jnp.dot(a, b, preferred_element_type=F32)


def dot_t(a, b):
    return lax.dot_general(a, b, (((0,), (0,)), ((), ())), preferred_element_type=F32)


def prep_kernel(ids_ref, tok_ref, place_ref, out_ref, *, peers):
    tokens = tok_ref.shape[0]
    width = tok_ref.shape[1]
    half = width // 2
    rows = peers * PACK
    before = (iota((tokens, tokens), 0) < iota((tokens, tokens), 1)).astype(BF16)
    experts = iota((peers, tokens), 0)
    first = experts == ids_ref[0:1, :]
    second = experts == ids_ref[1:2, :]
    first_f, second_f = first.astype(F32), second.astype(F32)
    rank0 = jnp.sum(dot(first.astype(BF16), before) * first_f, 0, keepdims=True)
    count0 = jnp.sum(first_f, 1, keepdims=True)
    rank1 = jnp.sum((dot(second.astype(BF16), before) + count0) * second_f, 0, keepdims=True)
    rank = jnp.concatenate([rank0, rank1], 0).astype(jnp.int32)
    base = ids_ref[...] * PACK + rank
    whole = jnp.where(rank < PACK, base, -rows)
    split = jnp.where(rank < PACK, -rows, base - PACK)
    place_ref[0:2, :] = whole
    place_ref[2:4, :] = split
    row = iota((rows, tokens), 0)
    pick = ((row == whole[0:1, :]) | (row == whole[1:2, :])).astype(BF16)
    left = ((row == split[0:1, :]) | (row == split[1:2, :])).astype(BF16)
    right = ((row == split[0:1, :] + EXTRA) | (row == split[1:2, :] + EXTRA)).astype(BF16)
    step = width // 7
    for c in range(0, width, step):
        out_ref[:, c : c + step] = dot(pick, tok_ref[:, c : c + step]).astype(BF16)
    step = half // 7
    for c in range(0, half, step):
        part = dot(left, tok_ref[:, c : c + step])
        part = part + dot(right, tok_ref[:, half + c : half + c + step])
        out_ref[:, width + c : width + c + step] = part.astype(BF16)


def prep(ids, tokens, peers):
    count, width = tokens.shape
    return pl.pallas_call(
        functools.partial(prep_kernel, peers=peers),
        out_shape=(
            jax.ShapeDtypeStruct((4, count), jnp.int32),
            jax.ShapeDtypeStruct((peers * PACK, width + width // 2), BF16),
        ),
        compiler_params=pltpu.CompilerParams(vmem_limit_bytes=40 * 2**20),
        name="dispatch_rows",
    )(ids, tokens)


def combine_kernel(place_ref, gate_ref, tok_ref, back_ref, out_ref):
    tokens, width = tok_ref.shape
    half = width // 2
    rows = back_ref.shape[0]
    row = iota((rows, tokens), 0)
    g0, g1 = gate_ref[0:1, :], gate_ref[1:2, :]

    def weights(p0, p1):
        return (jnp.where(row == p0, g0, 0.0) + jnp.where(row == p1, g1, 0.0)).astype(BF16)

    whole = weights(place_ref[0:1, :], place_ref[1:2, :])
    left = weights(place_ref[2:3, :], place_ref[3:4, :])
    right = weights(place_ref[2:3, :] + EXTRA, place_ref[3:4, :] + EXTRA)
    step = half // 7
    for side, extra in ((0, left), (1, right)):
        for c in range(0, half, step):
            at = side * half + c
            total = tok_ref[:, at : at + step].astype(F32)
            total = total + dot_t(whole, back_ref[:, at : at + step])
            total = total + dot_t(extra, back_ref[:, width + c : width + c + step])
            out_ref[:, at : at + step] = total.astype(BF16)


def combine(place, gates, tokens, back):
    return pl.pallas_call(
        combine_kernel,
        out_shape=jax.ShapeDtypeStruct(tokens.shape, BF16),
        compiler_params=pltpu.CompilerParams(vmem_limit_bytes=40 * 2**20),
        name="weighted_rows",
    )(place, gates, tokens, back)


def silu(v):
    return 0.5 * v * (1.0 + jnp.tanh(0.5 * v))


def expert_kernel(
    x_hbm, ia, ib, oa, ob, y_hbm, pack, x, wi, wo, h, y, y2, sx, si, so, sy, *, fw, dw, ahead
):
    rows, packed_width = pack.shape
    width = x.shape[1]
    more = x.shape[0] - rows
    hid = ia.shape[1]
    n1, n2 = hid // fw, width // dw

    def part(at, size):
        return pl.ds(pl.multiple_of(at * size, size), size)

    def for_tile(t, act):
        @pl.when(t < n1)
        def _():
            act(pltpu.make_async_copy(ia.at[:, part(t, fw)], wi.at[t], si.at[t]))

        @pl.when((t >= n1) & (t < 2 * n1))
        def _():
            act(pltpu.make_async_copy(ib.at[:, part(t - n1, fw)], wi.at[t], si.at[t]))

        @pl.when((t >= 2 * n1) & (t < 2 * n1 + n2))
        def _():
            j = t - 2 * n1
            for k, src in ((0, oa), (1, ob)):
                dst = wo.at[j, pl.ds(k * hid, hid)]
                act(pltpu.make_async_copy(src.at[:, part(j, dw)], dst, so.at[k, j]))

    def start(t):
        for_tile(t, lambda copy: copy.start())

    def wait(t):
        for_tile(t, lambda copy: copy.wait())

    fetch_pack = pltpu.make_async_copy(x_hbm.at[:, pl.ds(width, packed_width)], pack, sx.at[0])
    fetch = pltpu.make_async_copy(x_hbm.at[:, pl.ds(0, width)], x.at[pl.ds(0, rows)], sx.at[1])
    fetch_pack.start()
    fetch.start()

    @pl.loop(0, ahead)
    def _(t):
        start(t)

    fetch_pack.wait()
    source = iota((more, rows), 0) // EXTRA * PACK + iota((more, rows), 0) % EXTRA
    column = iota((more, rows), 1)
    x[rows:, :packed_width] = dot((source == column).astype(BF16), pack[...]).astype(BF16)
    x[rows:, packed_width:] = dot((source + EXTRA == column).astype(BF16), pack[...]).astype(BF16)
    fetch.wait()

    @pl.loop(0, 2 * n1)
    def _(t):
        start(t + ahead)
        wait(t)
        h[:, part(t, fw)] = silu(dot(x[...], wi[t])).astype(BF16)

    def store(j):
        return pltpu.make_async_copy(y.at[j], y_hbm.at[:, part(j, dw)], sy.at[j])

    @pl.loop(0, n2)
    def _(j):
        start(2 * n1 + j + ahead)
        wait(2 * n1 + j)
        y[j] = dot(h[:rows, :], wo[j]).astype(BF16)
        store(j).start()
        y2[:, part(j, dw)] = dot(h[rows:, :], wo[j]).astype(BF16)

    row = iota((rows, more), 0)
    origin = iota((rows, more), 1) // EXTRA * PACK + iota((rows, more), 1) % EXTRA
    left, right = (row == origin).astype(BF16), (row == origin + EXTRA).astype(BF16)
    pack[...] = (dot(left, y2[:, :packed_width]) + dot(right, y2[:, packed_width:])).astype(BF16)
    store_pack = pltpu.make_async_copy(pack, y_hbm.at[:, pl.ds(width, packed_width)], sx.at[0])
    store_pack.start()

    @pl.loop(0, n2)
    def _(j):
        store(j).wait()

    store_pack.wait()


def expert(x, own_in, other_in, own_out, other_out, fw=256, dw=512, ahead=3):
    width, hid = own_in.shape
    rows = x.shape[0]
    more = rows // PACK * EXTRA
    n1, n2 = hid // fw, width // dw
    anywhere = pl.BlockSpec(memory_space=pl.ANY)
    return pl.pallas_call(
        functools.partial(expert_kernel, fw=fw, dw=dw, ahead=ahead),
        out_shape=jax.ShapeDtypeStruct(x.shape, BF16),
        in_specs=[anywhere] * 5,
        out_specs=anywhere,
        scratch_shapes=[
            pltpu.VMEM((rows, width // 2), BF16),
            pltpu.VMEM((rows + more, width), BF16),
            pltpu.VMEM((2 * n1, width, fw), BF16),
            pltpu.VMEM((n2, 2 * hid, dw), BF16),
            pltpu.VMEM((rows + more, 2 * hid), BF16),
            pltpu.VMEM((n2, rows, dw), BF16),
            pltpu.VMEM((more, width), BF16),
            pltpu.SemaphoreType.DMA((2,)),
            pltpu.SemaphoreType.DMA((2 * n1,)),
            pltpu.SemaphoreType.DMA((2, n2)),
            pltpu.SemaphoreType.DMA((n2,)),
        ],
        compiler_params=pltpu.CompilerParams(vmem_limit_bytes=60 * 2**20),
        cost_estimate=pl.CostEstimate(
            flops=8 * (rows + more) * width * hid,
            bytes_accessed=8 * width * hid + 4 * x.size,
            transcendentals=2 * (rows + more) * hid,
        ),
        name="expert_layer",
    )(x, own_in, other_in, own_out, other_out)


def swap(x, peers):
    chunks = x.reshape(peers, x.shape[0] // peers, x.shape[1])
    return lax.all_to_all(chunks, "expert", split_axis=0, concat_axis=0, tiled=True).reshape(x.shape)


def per_device(tokens, expert_ids, gate_weights, w_in, w_out):
    peers = lax.axis_size("expert")
    cores = lax.axis_size("dp")
    turn = [(i, (i + 1) % cores) for i in range(cores)]
    other_in = lax.ppermute(w_in, "dp", turn)
    other_out = lax.ppermute(w_out, "dp", turn)
    first = lax.axis_index("dp") == 0

    def dispatch(ids, tokens):
        place, sent = prep(ids, tokens, peers)
        return place, swap(sent, peers)

    def blank(ids, tokens):
        shapes = jax.eval_shape(dispatch, ids, tokens)
        return tuple(jnp.zeros(s.shape, s.dtype) for s in shapes)

    routed = lax.cond(first, dispatch, blank, expert_ids.T, tokens)
    routed, other_in, other_out = lax.optimization_barrier((routed, other_in, other_out))
    place, arrived = lax.cond(
        first, lambda routed, ids, tokens: routed, lambda routed, ids, tokens: dispatch(ids, tokens),
        routed, expert_ids.T, tokens,
    )
    outgoing = expert(arrived, w_in[0], other_in[0], w_out[0], other_out[0])
    returned = swap(outgoing, peers)
    return combine(place, gate_weights.T, tokens, returned)


def solution(mesh):
    placed = (
        P(("dp", "expert"), None),
        P(("dp", "expert"), None),
        P(("dp", "expert"), None),
        P("expert", None, "dp"),
        P("expert", "dp", None),
    )
    return jax.shard_map(
        per_device, mesh=mesh, in_specs=placed, out_specs=P(("dp", "expert"), None), check_vma=False
    )
```

time: 217 us -> 175 us (0.81)
  blocking collectives: 153 us -> 102 us
  waiting for transfers between devices: 1.41 us -> 24.6 us
  between operations: 13.4 us -> 0.03 us
  Pallas kernels: 48.1 us -> 44.5 us
    all_to_all x2, blocking collectives: 153 us -> 102 us  [swap(): lax.all_to_all(chunks, 'expert', split_axis=0, concat_axis=0, tiled=True)]
    ppermute x0 -> x2, waiting for transfers between devices: none -> 24.6 us  [the longest x1 13.1 us: per_device(): other_out = lax.ppermute(w_out, 'dp', turn)]
    pallas_call x1, Pallas kernels: 40.4 us -> 37.4 us  [expert(): pl.pallas_call(functools.partial(expert_kernel, fw=fw, dw=dw, ahead=ahead...]
    another operation x0 -> x2, local copies, waits for them, and re-layouts: none -> 2.72 us
  transfers between devices with their start and end apart: 2 -> 2, of which waited for: 0 -> 2; matrix products, arithmetic and copies ran while one was open for 0% -> 2% of each run, Pallas kernels for 1% -> 0%
where the time goes in v2:
time: 175 us
  blocking collectives  102 us (58%)
  Pallas kernels  44.5 us (25%)
  waiting for transfers between devices  24.6 us (14%)
  local copies, waits for them, and re-layouts  2.74 us (2%)
    all_to_all x2, blocking collectives, swap(): lax.all_to_all(chunks, 'expert', split_axis=0, concat_axis=0, tiled=True)  102 us
    pallas_call x1, Pallas kernels, expert(): pl.pallas_call(functools.partial(expert_kernel, fw=fw, dw=dw, ahead=ahead...  37.4 us
    ppermute x1, waiting for transfers between devices, per_device(): other_out = lax.ppermute(w_out, 'dp', turn)  13.1 us
    ppermute x1, waiting for transfers between devices, per_device(): other_in = lax.ppermute(w_in, 'dp', turn)  11.5 us
    pallas_call x1, Pallas kernels, prep(): pl.pallas_call(functools.partial(prep_kernel, peers=peers), out_shape=(ja...  3.75 us
  transfers between devices with their start and end apart: 2, of which 2 were waited for; matrix products, arithmetic and copies ran while one was open for 2% of the time, Pallas kernels for 0%

profile of v2, /device:TPU:1, one launch (start us, length us, event | category | flops | bytes accessed | tf_op | source)
XLA Modules:
  0.0 174.9 jit_solution(18304611966555946399)
XLA Ops:
  0.0 1.4 collective-permute-start
  1.4 0.0 collective-permute-start.1
  1.4 2.7 %conditional.2 = (s32[4,256]{1,0:T(4,128)S(1)}, bf16[512,5376]{1,0:T(8,128)(2,1)}) conditional(s32[]{:T(128)} %convert_element_type.4, () %tuple.22, (s32[2,256]{1,0:T(2,128)}, bf16[256,3584]{1,0:T(8,128)(2,1)}) %tuple.31), branch_computations={%region_0.0_spmd, %region_1.0_spmd} | conditional | bytes 11010064 | solution.py:246
  1.4 2.7 %broadcast.5 = bf16[512,5376]{1,0:T(8,128)(2,1)} broadcast(bf16[]{:T(256)} %constant.3.clone), dimensions={} | broadcast | bytes 5505026 | tf_op jit(solution)/shard_map/broadcast.2
  4.2 11.5 %collective-permute-done = bf16[1,3584,1280]{2,1,0:T(8,128)(2,1)} collective-permute-done((bf16[1,3584,1280]{2,1,0:T(8,128)(2,1)}, bf16[1,3584,1280]{2,1,0:T(8,128)(2,1)}, u32[]{:S(2)}, u32[]{:S(2)}) %collective-permute-start) | collective-permute-done | bytes 9175072 | tf_op jit(solution)/shard_map/ppermute | solution.py:234
  15.7 13.1 %collective-permute-done.1 = bf16[1,1280,3584]{2,1,0:T(8,128)(2,1)} collective-permute-done((bf16[1,1280,3584]{2,1,0:T(8,128)(2,1)}, bf16[1,1280,3584]{2,1,0:T(8,128)(2,1)}, u32[]{:S(2)}, u32[]{:S(2)}) %collective-permute-start.1) | collective-permute-done | bytes 9175072 | tf_op jit(solution)/shard_map/ppermute | solution.py:235
  28.8 55.6 %conditional.3 = ((s32[4,256]{1,0:T(4,128)S(1)}, bf16[512,5376]{1,0:T(8,128)(2,1)})) conditional(s32[]{:T(128)} %convert_element_type.4, (s32[2,256]{1,0:T(2,128)}, bf16[256,3584]{1,0:T(8,128)(2,1)}) %tuple.32, (s32[4,256]{1,0:T(4,128)S(1)}, bf16[512,5376]{1,0:T(8,128)(2,1)}) %conditional.2), branch_computations={%region_2.0_spmd, %region_3.0_spmd} | conditional | bytes 11010072 | solution.py:248
  28.8 3.8 %dispatch_rows.3 = (s32[4,256]{1,0:T(4,128)S(1)}, bf16[512,5376]{1,0:T(8,128)(2,1)S(1)}) custom-call(s32[2,256]{1,0:T(2,128)} %get-tuple-element.21.ids_ref, bf16[256,3584]{1,0:T(8,128)(2,1)} %get-tuple-element.22.tok_ref), custom_call_target="tpu_custom_call" | custom-call | tf_op jit(solution)/shard_map/cond/branch_0_fun/dispatch_rows/pallas_call | solution.py:63
  32.6 51.9 %all_to_all.14 = bf16[64,8,5376]{2,1,0:T(8,128)(2,1)} all-to-all(bf16[64,8,5376]{2,1,0:T(8,128)(2,1)S(1)} %bitcast.13), channel_id=1, replica_groups=mesh['dp'=2,'expert'=64] {'expert'}, dimensions={0} | all-to-all | bytes 11010048 | tf_op jit(solution)/shard_map/cond/branch_0_fun/all_to_all | solution.py:227
  84.4 37.4 %expert_layer.1 = bf16[512,5376]{1,0:T(8,128)(2,1)} custom-call(bf16[512,5376]{1,0:T(8,128)(2,1)} %get-tuple-element.38.x_hbm, bf16[3584,1280]{1,0:T(8,128)(2,1)} %bitcast.19, bf16[3584,1280]{1,0:T(8,128)(2,1)} %bitcast.7.ib, bf16[1280,3584]{1,0:T(8,128)(2,1)} %bitcast.20, bf16[1280,3584]{1,0:T(8,128)(2,1)} %bitcast.9.ob), custom_call_target="tpu_custom_call" | custom-call | flops 28185722880 | bytes 47710208 | tf_op jit(solution)/shard_map/expert_layer/pallas_call | solution.py:197
  121.8 0.0 copy-start
  121.8 0.0 copy-start.1
  121.8 49.6 %all_to_all.15 = bf16[64,8,5376]{2,1,0:T(8,128)(2,1)S(1)} all-to-all(bf16[64,8,5376]{2,1,0:T(8,128)(2,1)} %bitcast.16), channel_id=1, replica_groups=mesh['dp'=2,'expert'=64] {'expert'}, dimensions={0} | all-to-all | bytes 11010048 | tf_op jit(solution)/shard_map/all_to_all | solution.py:227
  171.5 0.0 copy-done
  171.5 0.0 copy-done.1
  171.5 3.4 %weighted_rows.1 = bf16[256,3584]{1,0:T(8,128)(2,1)} custom-call(s32[4,256]{1,0:T(4,128)S(1)} %get-tuple-element.37.place_ref, f32[2,256]{1,0:T(2,128)S(1)} %bitcast.15, bf16[256,3584]{1,0:T(8,128)(2,1)S(1)} %copy-done.1, bf16[512,5376]{1,0:T(8,128)(2,1)S(1)} %bitcast.12), custom_call_target="tpu_custom_call" | custom-call | tf_op jit(solution)/shard_map/weighted_rows/pallas_call | solution.py:98
  (1 shorter events, 0.0 us)
Async XLA Ops:
  0.0 15.7 %collective-permute-start = (bf16[1,3584,1280]{2,1,0:T(8,128)(2,1)}, bf16[1,3584,1280]{2,1,0:T(8,128)(2,1)}, u32[]{:S(2)}, u32[]{:S(2)}) collective-permute-start(bf16[1,3584,1280]{2,1,0:T(8,128)(2,1)} %param.12), channel_id=1, source_target_pairs={{0,64},{64,0},{1,65},{65,1},{2,66},{66,2},{3,67},{67,3},{4,68},{68... | collective-permute-start | bytes 27525128 | tf_op jit(solution)/shard_map/ppermute | solution.py:234
  1.4 27.4 %collective-permute-start.1 = (bf16[1,1280,3584]{2,1,0:T(8,128)(2,1)}, bf16[1,1280,3584]{2,1,0:T(8,128)(2,1)}, u32[]{:S(2)}, u32[]{:S(2)}) collective-permute-start(bf16[1,1280,3584]{2,1,0:T(8,128)(2,1)} %param.13), channel_id=1, source_target_pairs={{0,64},{64,0},{1,65},{65,1},{2,66},{66,2},{3,67},{67,3},{4,68},{68... | collective-permute-start | bytes 27525128 | tf_op jit(solution)/shard_map/ppermute | solution.py:235
  121.8 49.7 %copy-start = (f32[256,2]{0,1:T(2,128)S(1)}, f32[256,2]{0,1:T(2,128)}, u32[]{:S(2)}) copy-start(f32[256,2]{0,1:T(2,128)} %param.11) | copy-start | bytes 6148
  121.8 49.7 %copy-start.1 = (bf16[256,3584]{1,0:T(8,128)(2,1)S(1)}, bf16[256,3584]{1,0:T(8,128)(2,1)}, u32[]{:S(2)}) copy-start(bf16[256,3584]{1,0:T(8,128)(2,1)} %tok_ref.1) | copy-start | bytes 5505028

commit v3 on v2

v3 whole, which is shorter than its diff:
```python
import functools

import jax
import jax.numpy as jnp
from jax import lax
from jax.experimental import pallas as pl
from jax.experimental.pallas import tpu as pltpu
from jax.sharding import PartitionSpec as P

PACK = 8
EXTRA = 4
BF16 = jnp.bfloat16
F32 = jnp.float32


def iota(shape, dim):
    return lax.broadcasted_iota(jnp.int32, shape, dim)


def dot(a, b):
    return jnp.dot(a, b, preferred_element_type=F32)


def dot_t(a, b):
    return lax.dot_general(a, b, (((0,), (0,)), ((), ())), preferred_element_type=F32)


def prep_kernel(ids_ref, tok_ref, place_ref, out_ref, *pack_refs, peers):
    tokens = tok_ref.shape[0]
    width = tok_ref.shape[1]
    half = width // 2
    rows = peers * PACK
    before = (iota((tokens, tokens), 0) < iota((tokens, tokens), 1)).astype(BF16)
    experts = iota((peers, tokens), 0)
    first = experts == ids_ref[0:1, :]
    second = experts == ids_ref[1:2, :]
    first_f, second_f = first.astype(F32), second.astype(F32)
    rank0 = jnp.sum(dot(first.astype(BF16), before) * first_f, 0, keepdims=True)
    count0 = jnp.sum(first_f, 1, keepdims=True)
    rank1 = jnp.sum((dot(second.astype(BF16), before) + count0) * second_f, 0, keepdims=True)
    rank = jnp.concatenate([rank0, rank1], 0).astype(jnp.int32)
    base = ids_ref[...] * PACK + rank
    whole = jnp.where(rank < PACK, base, -rows)
    split = jnp.where(rank < PACK, -rows, base - PACK)
    place_ref[0:2, :] = whole
    place_ref[2:4, :] = split
    row = iota((rows, tokens), 0)
    pick = ((row == whole[0:1, :]) | (row == whole[1:2, :])).astype(BF16)
    left = ((row == split[0:1, :]) | (row == split[1:2, :])).astype(BF16)
    right = ((row == split[0:1, :] + EXTRA) | (row == split[1:2, :] + EXTRA)).astype(BF16)
    step = width // 7
    for c in range(0, width, step):
        out_ref[:, c : c + step] = dot(pick, tok_ref[:, c : c + step]).astype(BF16)
    step = half // 7
    for c in range(0, half, step):
        part = dot(left, tok_ref[:, c : c + step])
        part = part + dot(right, tok_ref[:, half + c : half + c + step])
        if pack_refs:
            pack_refs[0][:, c : c + step] = part.astype(BF16)
        else:
            out_ref[:, width + c : width + c + step] = part.astype(BF16)


def prep(ids, tokens, peers, apart):
    count, width = tokens.shape
    pack = (jax.ShapeDtypeStruct((peers * PACK, width // 2), BF16),) if apart else ()
    sent = width if apart else width + width // 2
    return pl.pallas_call(
        functools.partial(prep_kernel, peers=peers),
        out_shape=(
            jax.ShapeDtypeStruct((4, count), jnp.int32),
            jax.ShapeDtypeStruct((peers * PACK, sent), BF16),
        )
        + pack,
        compiler_params=pltpu.CompilerParams(vmem_limit_bytes=40 * 2**20),
        name="dispatch_rows",
    )(ids, tokens)


def combine_kernel(place_ref, gate_ref, tok_ref, back_ref, pack_ref, out_ref):
    tokens, width = tok_ref.shape
    half = width // 2
    rows = back_ref.shape[0]
    row = iota((rows, tokens), 0)
    g0, g1 = gate_ref[0:1, :], gate_ref[1:2, :]

    def weights(p0, p1):
        return (jnp.where(row == p0, g0, 0.0) + jnp.where(row == p1, g1, 0.0)).astype(BF16)

    whole = weights(place_ref[0:1, :], place_ref[1:2, :])
    left = weights(place_ref[2:3, :], place_ref[3:4, :])
    right = weights(place_ref[2:3, :] + EXTRA, place_ref[3:4, :] + EXTRA)
    step = half // 7
    for side, extra in ((0, left), (1, right)):
        for c in range(0, half, step):
            at = side * half + c
            total = tok_ref[:, at : at + step].astype(F32)
            total = total + dot_t(whole, back_ref[:, at : at + step])
            total = total + dot_t(extra, pack_ref[:, c : c + step])
            out_ref[:, at : at + step] = total.astype(BF16)


def combine(place, gates, tokens, whole, pack, room):
    count, width = tokens.shape
    rows = whole.shape[0]

    def block(shape, at=0):
        return pl.BlockSpec(shape, lambda i: (0, at))

    return pl.pallas_call(
        combine_kernel,
        out_shape=jax.ShapeDtypeStruct(tokens.shape, BF16),
        grid=(1,),
        in_specs=[
            block(place.shape),
            block(gates.shape),
            block(tokens.shape),
            block((rows, width)),
            block((rows, width // 2), 2 if pack.shape[1] > width // 2 else 0),
        ],
        out_specs=block(tokens.shape),
        compiler_params=pltpu.CompilerParams(vmem_limit_bytes=room * 2**20),
        name="weighted_rows",
    )(place, gates, tokens, whole, pack)


def gate_weights_of(row, place, gate):
    w = jnp.where(row == place[0:1, :], gate[0:1, :], 0.0)
    return (w + jnp.where(row == place[1:2, :], gate[1:2, :], 0.0)).astype(BF16)


def sum_whole_kernel(place_ref, gate_ref, tok_ref, back_ref, out_ref):
    tokens, width = tok_ref.shape
    row = iota((back_ref.shape[0], tokens), 0)
    whole = gate_weights_of(row, place_ref[0:2, :], gate_ref[...])
    step = width // 14
    for c in range(0, width, step):
        out_ref[:, c : c + step] = tok_ref[:, c : c + step].astype(F32) + dot_t(whole, back_ref[:, c : c + step])


def sum_packed_kernel(place_ref, gate_ref, part_ref, pack_ref, out_ref):
    tokens, width = part_ref.shape
    half = width // 2
    row = iota((pack_ref.shape[0], tokens), 0)
    step = half // 7
    for side in range(2):
        extra = gate_weights_of(row, place_ref[2:4, :] + EXTRA * side, gate_ref[...])
        for c in range(0, half, step):
            at = side * half + c
            total = part_ref[:, at : at + step] + dot_t(extra, pack_ref[:, c : c + step])
            out_ref[:, at : at + step] = total.astype(BF16)


def add_rows(kernel, place, gates, base, back, out_type, name):
    count, width = base.shape
    rows = back.shape[0]

    def block(shape):
        return pl.BlockSpec(shape, lambda i: (0, 0))

    return pl.pallas_call(
        kernel,
        out_shape=jax.ShapeDtypeStruct(base.shape, out_type),
        grid=(1,),
        in_specs=[
            block(place.shape),
            block(gates.shape),
            block(base.shape),
            block((rows, min(width, back.shape[1]))),
        ],
        out_specs=block(base.shape),
        compiler_params=pltpu.CompilerParams(vmem_limit_bytes=32 * 2**20),
        cost_estimate=pl.CostEstimate(
            flops=2 * rows * base.size, bytes_accessed=12 * base.size, transcendentals=0
        ),
        name=name,
    )(place, gates, base, back)


def silu(v):
    return 0.5 * v * (1.0 + jnp.tanh(0.5 * v))


def expert_kernel(
    x_hbm, ia, ib, oa, ob, *refs, whole, packed, fw, dw, ahead
):
    y_hbm, pack, x, wi, wo, h, y, y2, sx, si, so, sy = refs[-12:]
    wire = x_hbm.shape[0]
    width = x.shape[1]
    half = width // 2
    rows = wire if whole else 0
    more = x.shape[0] - rows
    hid = ia.shape[1]
    n1, n2 = hid // fw, width // dw
    beside = refs[0] if len(refs) > 12 else None

    def part(at, size):
        return pl.ds(pl.multiple_of(at * size, size), size)

    def for_tile(t, act):
        @pl.when(t < n1)
        def _():
            act(pltpu.make_async_copy(ia.at[:, part(t, fw)], wi.at[t], si.at[t]))

        @pl.when((t >= n1) & (t < 2 * n1))
        def _():
            act(pltpu.make_async_copy(ib.at[:, part(t - n1, fw)], wi.at[t], si.at[t]))

        @pl.when((t >= 2 * n1) & (t < 2 * n1 + n2))
        def _():
            j = t - 2 * n1
            for k, src in ((0, oa), (1, ob)):
                dst = wo.at[j, pl.ds(k * hid, hid)]
                act(pltpu.make_async_copy(src.at[:, part(j, dw)], dst, so.at[k, j]))

    def start(t):
        for_tile(t, lambda copy: copy.start())

    def wait(t):
        for_tile(t, lambda copy: copy.wait())

    if packed:
        columns = pl.ds(width, half)
        fetch_pack = pltpu.make_async_copy(x_hbm.at[:, columns], pack, sx.at[0])
        fetch_pack.start()
    if whole:
        columns = pl.ds(0, width)
        fetch = pltpu.make_async_copy(x_hbm.at[:, columns], x.at[pl.ds(0, rows)], sx.at[1])
        fetch.start()

    @pl.loop(0, ahead)
    def _(t):
        start(t)

    if beside is not None:
        bring = pltpu.make_async_copy(beside, pack, sx.at[0])
        bring.start()
    if packed:
        fetch_pack.wait()
        source = iota((more, wire), 0) // EXTRA * PACK + iota((more, wire), 0) % EXTRA
        column = iota((more, wire), 1)
        x[rows:, :half] = dot((source == column).astype(BF16), pack[...]).astype(BF16)
        x[rows:, half:] = dot((source + EXTRA == column).astype(BF16), pack[...]).astype(BF16)
    if whole:
        fetch.wait()

    @pl.loop(0, 2 * n1)
    def _(t):
        start(t + ahead)
        wait(t)
        h[:, part(t, fw)] = silu(dot(x[...], wi[t])).astype(BF16)

    if beside is not None:
        bring.wait()
        leave = pltpu.make_async_copy(pack, y_hbm.at[:, pl.ds(width, half)], sx.at[0])
        leave.start()

    def store(j):
        return pltpu.make_async_copy(y.at[j], y_hbm.at[:, part(j, dw)], sy.at[j])

    @pl.loop(0, n2)
    def _(j):
        start(2 * n1 + j + ahead)
        wait(2 * n1 + j)
        if whole:
            y[j] = dot(h[:rows, :], wo[j]).astype(BF16)
            store(j).start()
        if packed:
            y2[:, part(j, dw)] = dot(h[rows:, :], wo[j]).astype(BF16)

    if packed:
        row = iota((wire, more), 0)
        origin = iota((wire, more), 1) // EXTRA * PACK + iota((wire, more), 1) % EXTRA
        left, right = (row == origin).astype(BF16), (row == origin + EXTRA).astype(BF16)
        pack[...] = (dot(left, y2[:, :half]) + dot(right, y2[:, half:])).astype(BF16)
        columns = pl.ds(width if whole else 0, half)
        store_pack = pltpu.make_async_copy(pack, y_hbm.at[:, columns], sx.at[0])
        store_pack.start()
    if whole:

        @pl.loop(0, n2)
        def _(j):
            store(j).wait()

    if packed:
        store_pack.wait()
    if beside is not None:
        leave.wait()


def expert(x, weights, whole, packed, beside=None, fw=256, dw=512, ahead=3):
    width, hid = weights[0].shape
    wire = x.shape[0]
    rows = (wire if whole else 0) + (wire // PACK * EXTRA if packed else 0)
    n1, n2 = hid // fw, width // dw
    anywhere = pl.BlockSpec(memory_space=pl.ANY)
    args = (x,) + tuple(weights) + (() if beside is None else (beside,))
    out = (width if whole else 0) + (width // 2 if packed or beside is not None else 0)
    spare = (16, 128)
    return pl.pallas_call(
        functools.partial(expert_kernel, whole=whole, packed=packed, fw=fw, dw=dw, ahead=ahead),
        out_shape=jax.ShapeDtypeStruct((wire, out), BF16),
        in_specs=[anywhere] * len(args),
        out_specs=anywhere,
        scratch_shapes=[
            pltpu.VMEM((wire, width // 2) if packed or beside is not None else spare, BF16),
            pltpu.VMEM((rows, width), BF16),
            pltpu.VMEM((2 * n1, width, fw), BF16),
            pltpu.VMEM((n2, 2 * hid, dw), BF16),
            pltpu.VMEM((rows, 2 * hid), BF16),
            pltpu.VMEM((n2, wire, dw) if whole else (1,) + spare, BF16),
            pltpu.VMEM((wire // PACK * EXTRA, width) if packed else spare, BF16),
            pltpu.SemaphoreType.DMA((2,)),
            pltpu.SemaphoreType.DMA((2 * n1,)),
            pltpu.SemaphoreType.DMA((2, n2)),
            pltpu.SemaphoreType.DMA((n2,)),
        ],
        compiler_params=pltpu.CompilerParams(vmem_limit_bytes=60 * 2**20),
        cost_estimate=pl.CostEstimate(
            flops=8 * rows * width * hid,
            bytes_accessed=8 * width * hid + 4 * rows * width,
            transcendentals=2 * rows * hid,
        ),
        name="expert_whole" if not packed else "expert_both" if whole else "expert_packed",
    )(*args)


def unused(shape, after):
    anywhere = pl.BlockSpec(memory_space=pl.ANY)
    return pl.pallas_call(
        lambda after, out: None,
        out_shape=jax.ShapeDtypeStruct(shape, BF16),
        in_specs=[anywhere],
        out_specs=anywhere,
        name="unused",
    )(after)


def swap(x, peers):
    chunks = x.reshape(peers, x.shape[0] // peers, x.shape[1])
    return lax.all_to_all(chunks, "expert", split_axis=0, concat_axis=0, tiled=True).reshape(x.shape)


def per_device(tokens, expert_ids, gate_weights, w_in, w_out):
    peers = lax.axis_size("expert")
    cores = lax.axis_size("dp")
    turn = [(i, (i + 1) % cores) for i in range(cores)]
    other_in = lax.ppermute(w_in, "dp", turn)
    other_out = lax.ppermute(w_out, "dp", turn)
    first = lax.axis_index("dp") == 0

    def send_whole(ids, tokens):
        place, sent, pack = prep(ids, tokens, peers, apart=True)
        arrived = swap(sent, peers)
        return place, arrived, pack, unused((sent.shape[0], sent.shape[1] + pack.shape[1]), arrived)

    def send_later(ids, tokens):
        place, sent = prep(ids, tokens, peers, apart=False)
        rows, width = sent.shape[0], tokens.shape[1]
        return place, unused((rows, width), sent), unused((rows, width // 2), sent), sent

    def two_parts(routed, gates, tokens, weights):
        place, arrived, pack, _ = routed
        mixed = swap(expert(arrived, weights, whole=True, packed=False, beside=pack), peers)
        back = swap(expert(mixed, weights, whole=False, packed=True), peers)
        part = add_rows(sum_whole_kernel, place, gates, tokens, mixed, F32, "sum_whole")
        return add_rows(sum_packed_kernel, place, gates, part, back, BF16, "sum_packed")

    def one_part(routed, gates, tokens, weights):
        place, _, _, sent = routed
        back = swap(expert(swap(sent, peers), weights, whole=True, packed=True), peers)
        return combine(place, gates, tokens, back, back, 40)

    routed = lax.cond(first, send_whole, send_later, expert_ids.T, tokens)
    routed, other_in, other_out = lax.optimization_barrier((routed, other_in, other_out))
    weights = (w_in[0], other_in[0], w_out[0], other_out[0])
    return lax.cond(first, two_parts, one_part, routed, gate_weights.T, tokens, weights)


def solution(mesh):
    placed = (
        P(("dp", "expert"), None),
        P(("dp", "expert"), None),
        P(("dp", "expert"), None),
        P("expert", None, "dp"),
        P("expert", "dp", None),
    )
    return jax.shard_map(
        per_device, mesh=mesh, in_specs=placed, out_specs=P(("dp", "expert"), None), check_vma=False
    )
```

time: 175 us -> 171 us (0.977)
  waiting for transfers between devices: 24.6 us -> 21.2 us
    ppermute x1, waiting for transfers between devices: 11.5 us -> 8.06 us  [per_device(): other_in = lax.ppermute(w_in, 'dp', turn)]
    another operation x2 -> x0, local copies, waits for them, and re-layouts: 2.72 us -> none
    pallas_call x1, Pallas kernels: 3.75 us -> 6.18 us  [prep(): pl.pallas_call(functools.partial(prep_kernel, peers=peers), out_shape=(ja...]
    pallas_call x1 -> x3, Pallas kernels: 37.4 us -> 37.4 us  [the longest x1 37.4 us: expert(): pl.pallas_call(functools.partial(expert_kernel, whole=whole, packed=packe...]
  transfers between devices with their start and end apart: 2 -> 2, of which waited for: 2 -> 2; matrix products, arithmetic and copies ran while one was open for 2% -> 0% of each run, Pallas kernels for 0% -> 4%
where the time goes in v3:
time: 171 us
  blocking collectives  101 us (59%)
  Pallas kernels  45.8 us (27%)
  waiting for transfers between devices  21.2 us (12%)
    all_to_all x2, blocking collectives, swap(): lax.all_to_all(chunks, 'expert', split_axis=0, concat_axis=0, tiled=True)  101 us
    pallas_call x1, Pallas kernels, expert(): pl.pallas_call(functools.partial(expert_kernel, whole=whole, packed=packe...  37.4 us
    ppermute x1, waiting for transfers between devices, per_device(): other_out = lax.ppermute(w_out, 'dp', turn)  13.1 us
    ppermute x1, waiting for transfers between devices, per_device(): other_in = lax.ppermute(w_in, 'dp', turn)  8.06 us
    pallas_call x1, Pallas kernels, prep(): pl.pallas_call(functools.partial(prep_kernel, peers=peers), out_shape=(ja...  6.18 us
  transfers between devices with their start and end apart: 2, of which 2 were waited for; matrix products, arithmetic and copies ran while one was open for 0% of the time, Pallas kernels for 4%

profile of v3, /device:TPU:1, one launch (start us, length us, event | category | flops | bytes accessed | tf_op | source)
XLA Modules:
  0.0 170.8 jit_solution(9034405651351510042)
XLA Ops:
  0.0 1.4 collective-permute-start
  1.4 0.0 collective-permute-start.1
  1.4 0.0 copy-start.5
  1.4 6.2 %conditional.2 = (s32[4,256]{1,0:T(4,128)S(1)}, bf16[512,3584]{1,0:T(8,128)(2,1)}, bf16[512,1792]{1,0:T(8,128)(2,1)S(1)}, bf16[512,5376]{1,0:T(8,128)(2,1)}) conditional(s32[]{:T(128)} %convert_element_type.4, (s32[2,256]{1,0:T(2,128)}, bf16[256,3584]{1,0:T(8,128)(2,1)}) %tuple.37, (s32[2,256]{1,0:T(2,128)}, bf16[256,3584]{1,0:T(8,128)(2,1)}) %tuple.38), branch_computations={%region_0.0_spmd, %region_1.0_spmd} | conditional | bytes 7340064 | solution.py:374
  1.4 6.2 %dispatch_rows.2 = (s32[4,256]{1,0:T(4,128)S(1)}, bf16[512,5376]{1,0:T(8,128)(2,1)}) custom-call(s32[2,256]{1,0:T(2,128)} %get-tuple-element.50.ids_ref, bf16[256,3584]{1,0:T(8,128)(2,1)} %get-tuple-element.51.tok_ref), custom_call_target="tpu_custom_call" | custom-call | tf_op jit(solution)/shard_map/cond/branch_0_fun/dispatch_rows/pallas_call | solution.py:68
  7.6 8.1 %collective-permute-done = bf16[1,3584,1280]{2,1,0:T(8,128)(2,1)} collective-permute-done((bf16[1,3584,1280]{2,1,0:T(8,128)(2,1)}, bf16[1,3584,1280]{2,1,0:T(8,128)(2,1)}, u32[]{:S(2)}, u32[]{:S(2)}) %collective-permute-start) | collective-permute-done | bytes 9175072 | tf_op jit(solution)/shard_map/ppermute | solution.py:348
  15.7 13.1 %collective-permute-done.1 = bf16[1,1280,3584]{2,1,0:T(8,128)(2,1)} collective-permute-done((bf16[1,1280,3584]{2,1,0:T(8,128)(2,1)}, bf16[1,1280,3584]{2,1,0:T(8,128)(2,1)}, u32[]{:S(2)}, u32[]{:S(2)}) %collective-permute-start.1) | collective-permute-done | bytes 9175072 | tf_op jit(solution)/shard_map/ppermute | solution.py:349
  28.8 0.0 copy-done.5
  28.8 140.7 %conditional.3 = (bf16[256,3584]{1,0:T(8,128)(2,1)S(1)}) conditional(s32[]{:T(128)} %convert_element_type.4, (bf16[512,5376]{1,0:T(8,128)(2,1)}, bf16[3584,1280]{1,0:T(8,128)(2,1)}, bf16[3584,1280]{1,0:T(8,128)(2,1)}, bf16[1280,3584]{1,0:T(8,128)(2,1)}, bf16[1280,3584]{1,0:T(8,128)(2,1)}, /*index=5*/s32[4,256]{1,0:T(4,128)S(1)}, ...), branch_computations={%region_2.0_spmd, %region_3.0_spmd} | conditional | flops 30064771072 | bytes 174325888 | solution.py:377
  28.8 48.7 %all_to_all.21 = bf16[64,8,5376]{2,1,0:T(8,128)(2,1)} all-to-all(bf16[64,8,5376]{2,1,0:T(8,128)(2,1)} %bitcast.22), channel_id=1, replica_groups=mesh['dp'=2,'expert'=64] {'expert'}, dimensions={0} | all-to-all | bytes 11010048 | tf_op jit(solution)/shard_map/cond/branch_0_fun/all_to_all | solution.py:341
  77.5 37.4 %expert_both.1 = bf16[512,5376]{1,0:T(8,128)(2,1)} custom-call(bf16[512,5376]{1,0:T(8,128)(2,1)} %bitcast.31, bf16[3584,1280]{1,0:T(8,128)(2,1)} %get-tuple-element.63.ia, bf16[3584,1280]{1,0:T(8,128)(2,1)} %get-tuple-element.64.ib, bf16[1280,3584]{1,0:T(8,128)(2,1)} %get-tuple-element.65.oa, bf16[1280,3584]{1,0:T(8,128)(2,1)} %get-tuple-element.66.ob), custom_call_target="tpu_custom_call" | custom-call | flops 28185722880 | bytes 47710208 | tf_op jit(solution)/shard_map/cond/branch_0_fun/expert_both/pallas_call | solution.py:300
  114.9 0.0 copy-start.3
  115.0 52.2 %all_to_all.22 = bf16[64,8,5376]{2,1,0:T(8,128)(2,1)S(1)} all-to-all(bf16[64,8,5376]{2,1,0:T(8,128)(2,1)} %bitcast.30), channel_id=1, replica_groups=mesh['dp'=2,'expert'=64] {'expert'}, dimensions={0} | all-to-all | bytes 11010048 | tf_op jit(solution)/shard_map/cond/branch_0_fun/all_to_all | solution.py:341
  167.2 0.0 copy-done.3
  167.2 2.2 %weighted_rows.1 = bf16[256,3584]{1,0:T(8,128)(2,1)S(1)} custom-call(s32[4,256]{1,0:T(4,128)S(1)} %get-tuple-element.59.place_ref, f32[2,256]{1,0:T(2,128)S(1)} %get-tuple-element.60.gate_ref, bf16[256,3584]{1,0:T(8,128)(2,1)S(1)} %copy-done.3, bf16[512,5376]{1,0:T(8,128)(2,1)S(1)} %bitcast.16, bf16[512,5376]{1,0:T(8,128)(2,1)S(1)} %bitcast.17), custom_call_target="tpu_custom_call" | custom-call | tf_op jit(solution)/shard_map/cond/branch_0_fun/weighted_rows/pallas_call | solution.py:110
  169.5 0.0 copy-start.4
  169.6 1.2 copy-done.4
  (2 shorter events, 0.0 us)
Async XLA Ops:
  0.0 15.7 %collective-permute-start = (bf16[1,3584,1280]{2,1,0:T(8,128)(2,1)}, bf16[1,3584,1280]{2,1,0:T(8,128)(2,1)}, u32[]{:S(2)}, u32[]{:S(2)}) collective-permute-start(bf16[1,3584,1280]{2,1,0:T(8,128)(2,1)} %param.12), channel_id=1, source_target_pairs={{0,64},{64,0},{1,65},{65,1},{2,66},{66,2},{3,67},{67,3},{4,68},{68... | collective-permute-start | bytes 27525128 | tf_op jit(solution)/shard_map/ppermute | solution.py:348
  1.4 27.4 %collective-permute-start.1 = (bf16[1,1280,3584]{2,1,0:T(8,128)(2,1)}, bf16[1,1280,3584]{2,1,0:T(8,128)(2,1)}, u32[]{:S(2)}, u32[]{:S(2)}) collective-permute-start(bf16[1,1280,3584]{2,1,0:T(8,128)(2,1)} %param.13), channel_id=1, source_target_pairs={{0,64},{64,0},{1,65},{65,1},{2,66},{66,2},{3,67},{67,3},{4,68},{68... | collective-permute-start | bytes 27525128 | tf_op jit(solution)/shard_map/ppermute | solution.py:349
  1.4 27.4 %copy-start.5 = (f32[256,2]{0,1:T(2,128)S(1)}, f32[256,2]{0,1:T(2,128)}, u32[]{:S(2)}) copy-start(f32[256,2]{0,1:T(2,128)} %param.11) | copy-start | bytes 6148
  114.9 52.2 %copy-start.3 = (bf16[256,3584]{1,0:T(8,128)(2,1)S(1)}, bf16[256,3584]{1,0:T(8,128)(2,1)}, u32[]{:S(2)}) copy-start(bf16[256,3584]{1,0:T(8,128)(2,1)} %get-tuple-element.61.tok_ref) | copy-start | bytes 5505028 | tf_op jit(solution)/shard_map/cond
  169.5 1.2 copy-start.4

commit v4 on v3

--- a/solution.py
+++ b/solution.py
@@ -77,32 +77,41 @@
     )(ids, tokens)
 
 
-def combine_kernel(place_ref, gate_ref, tok_ref, back_ref, pack_ref, out_ref):
-    tokens, width = tok_ref.shape
+def gate_matrix_kernel(place_ref, gate_ref, after, out_ref):
+    rows, tokens = out_ref.shape[1:]
+    row = iota((rows, tokens), 0)
+    out_ref[0] = gate_weights_of(row, place_ref[0:2, :], gate_ref[...])
+    for side in range(2):
+        out_ref[1 + side] = gate_weights_of(row, place_ref[2:4, :] + EXTRA * side, gate_ref[...])
+
+
+def gate_matrices(place, gates, after):
+    inside, anywhere = pl.BlockSpec(memory_space=pltpu.VMEM), pl.BlockSpec(memory_space=pl.ANY)
+    return pl.pallas_call(
+        gate_matrix_kernel,
+        out_shape=jax.ShapeDtypeStruct((3, after.shape[0], place.shape[1]), BF16),
+        in_specs=[inside, inside, anywhere],
+        compiler_params=pltpu.CompilerParams(vmem_limit_bytes=32 * 2**20),
+        name="gate_matrices",
+    )(place, gates, after)
+
+
+def combine_kernel(weight_ref, tok_ref, back_ref, pack_ref, out_ref):
+    width = tok_ref.shape[1]
     half = width // 2
-    rows = back_ref.shape[0]
-    row = iota((rows, tokens), 0)
-    g0, g1 = gate_ref[0:1, :], gate_ref[1:2, :]
-
-    def weights(p0, p1):
-        return (jnp.where(row == p0, g0, 0.0) + jnp.where(row == p1, g1, 0.0)).astype(BF16)
-
-    whole = weights(place_ref[0:1, :], place_ref[1:2, :])
-    left = weights(place_ref[2:3, :], place_ref[3:4, :])
-    right = weights(place_ref[2:3, :] + EXTRA, place_ref[3:4, :] + EXTRA)
     step = half // 7
-    for side, extra in ((0, left), (1, right)):
+    for side in range(2):
         for c in range(0, half, step):
             at = side * half + c
             total = tok_ref[:, at : at + step].astype(F32)
-            total = total + dot_t(whole, back_ref[:, at : at + step])
-            total = total + dot_t(extra, pack_ref[:, c : c + step])
+            total = total + dot_t(weight_ref[0], back_ref[:, at : at + step])
+            total = total + dot_t(weight_ref[1 + side], pack_ref[:, c : c + step])
             out_ref[:, at : at + step] = total.astype(BF16)
 
 
-def combine(place, gates, tokens, whole, pack, room):
-    count, width = tokens.shape
-    rows = whole.shape[0]
+def combine(weight, tokens, back):
+    width = tokens.shape[1]
+    rows = back.shape[0]
 
     def block(shape, at=0):
         return pl.BlockSpec(shape, lambda i: (0, at))
@@ -112,16 +121,15 @@
         out_shape=jax.ShapeDtypeStruct(tokens.shape, BF16),
         grid=(1,),
         in_specs=[
-            block(place.shape),
-            block(gates.shape),
+            pl.BlockSpec(weight.shape, lambda i: (0, 0, 0)),
             block(tokens.shape),
             block((rows, width)),
-            block((rows, width // 2), 2 if pack.shape[1] > width // 2 else 0),
+            block((rows, width // 2), 2),
         ],
         out_specs=block(tokens.shape),
-        compiler_params=pltpu.CompilerParams(vmem_limit_bytes=room * 2**20),
+        compiler_params=pltpu.CompilerParams(vmem_limit_bytes=40 * 2**20),
         name="weighted_rows",
-    )(place, gates, tokens, whole, pack)
+    )(weight, tokens, back, back)
 
 
 def gate_weights_of(row, place, gate):
@@ -135,7 +143,8 @@
     whole = gate_weights_of(row, place_ref[0:2, :], gate_ref[...])
     step = width // 14
     for c in range(0, width, step):
-        out_ref[:, c : c + step] = tok_ref[:, c : c + step].astype(F32) + dot_t(whole, back_ref[:, c : c + step])
+        total = tok_ref[:, c : c + step].astype(F32) + dot_t(whole, back_ref[:, c : c + step])
+        out_ref[:, c : c + step] = total.astype(BF16)
 
 
 def sum_packed_kernel(place_ref, gate_ref, part_ref, pack_ref, out_ref):
@@ -147,7 +156,7 @@
         extra = gate_weights_of(row, place_ref[2:4, :] + EXTRA * side, gate_ref[...])
         for c in range(0, half, step):
             at = side * half + c
-            total = part_ref[:, at : at + step] + dot_t(extra, pack_ref[:, c : c + step])
+            total = part_ref[:, at : at + step].astype(F32) + dot_t(extra, pack_ref[:, c : c + step])
             out_ref[:, at : at + step] = total.astype(BF16)
 
 
@@ -363,13 +372,14 @@
         place, arrived, pack, _ = routed
         mixed = swap(expert(arrived, weights, whole=True, packed=False, beside=pack), peers)
         back = swap(expert(mixed, weights, whole=False, packed=True), peers)
-        part = add_rows(sum_whole_kernel, place, gates, tokens, mixed, F32, "sum_whole")
+        part = add_rows(sum_whole_kernel, place, gates, tokens, mixed, BF16, "sum_whole")
         return add_rows(sum_packed_kernel, place, gates, part, back, BF16, "sum_packed")
 
     def one_part(routed, gates, tokens, weights):
         place, _, _, sent = routed
-        back = swap(expert(swap(sent, peers), weights, whole=True, packed=True), peers)
-        return combine(place, gates, tokens, back, back, 40)
+        outgoing = expert(swap(sent, peers), weights, whole=True, packed=True)
+        back = swap(outgoing, peers)
+        return combine(gate_matrices(place, gates, outgoing), tokens, back)
 
     routed = lax.cond(first, send_whole, send_later, expert_ids.T, tokens)
     routed, other_in, other_out = lax.optimization_barrier((routed, other_in, other_out))

time: 171 us -> 176 us (1.029)
  blocking collectives: 101 us -> 48.7 us
  waiting for transfers between devices: 21.2 us -> 66.8 us
  starting transfers between devices: 1.42 us -> 7.44 us
  Pallas kernels: 45.8 us -> 48.6 us
  local copies, waits for them, and re-layouts: 1.23 us -> 3.82 us
    all_to_all x2 -> x1, blocking collectives: 101 us -> 48.7 us  [swap(): lax.all_to_all(chunks, 'expert', split_axis=0, concat_axis=0, tiled=True)]
    all_to_all x0 -> x1, waiting for transfers between devices: none -> 45.6 us  [swap(): lax.all_to_all(chunks, 'expert', split_axis=0, concat_axis=0, tiled=True)]
    all_to_all x0 -> x1, starting transfers between devices: none -> 6.02 us  [swap(): lax.all_to_all(chunks, 'expert', split_axis=0, concat_axis=0, tiled=True)]
    cond x2 -> x4, local copies, waits for them, and re-layouts: 0.01 us -> 2.59 us
    pallas_call x1, Pallas kernels: 2.17 us -> 4.73 us  [combine(): pl.pallas_call(combine_kernel, out_shape=jax.ShapeDtypeStruct(tokens.shap...]
  transfers between devices with their start and end apart: 2 -> 3, of which waited for: 2 -> 3; matrix products, arithmetic and copies ran while one was open for 0% -> 0% of each run, Pallas kernels for 4% -> 4%
where the time goes in v4:
time: 176 us
  waiting for transfers between devices  66.8 us (38%)
  blocking collectives  48.7 us (28%)
  Pallas kernels  48.6 us (28%)
  starting transfers between devices  7.44 us (4%)
  local copies, waits for them, and re-layouts  3.82 us (2%)
    all_to_all x1, blocking collectives, swap(): lax.all_to_all(chunks, 'expert', split_axis=0, concat_axis=0, tiled=True)  48.7 us
    all_to_all x1, waiting for transfers between devices, swap(): lax.all_to_all(chunks, 'expert', split_axis=0, concat_axis=0, tiled=True)  45.6 us
    pallas_call x1, Pallas kernels, expert(): pl.pallas_call(functools.partial(expert_kernel, whole=whole, packed=packe...  37.4 us
    ppermute x1, waiting for transfers between devices, per_device(): other_out = lax.ppermute(w_out, 'dp', turn)  13.1 us
    ppermute x1, waiting for transfers between devices, per_device(): other_in = lax.ppermute(w_in, 'dp', turn)  8.11 us
    pallas_call x1, Pallas kernels, prep(): pl.pallas_call(functools.partial(prep_kernel, peers=peers), out_shape=(ja...  6.13 us
    all_to_all x1, starting transfers between devices, swap(): lax.all_to_all(chunks, 'expert', split_axis=0, concat_axis=0, tiled=True)  6.02 us
    pallas_call x1, Pallas kernels, combine(): pl.pallas_call(combine_kernel, out_shape=jax.ShapeDtypeStruct(tokens.shap...  4.73 us
  transfers between devices with their start and end apart: 3, of which 3 were waited for; matrix products, arithmetic and copies ran while one was open for 0% of the time, Pallas kernels for 4%

profile of v4, /device:TPU:1, one launch (start us, length us, event | category | flops | bytes accessed | tf_op | source)
XLA Modules:
  0.0 175.6 jit_solution(5399133490406911976)
XLA Ops:
  0.0 1.4 collective-permute-start
  1.4 0.0 collective-permute-start.1
  1.4 0.0 copy-start.4
  1.4 6.1 %conditional.2 = (s32[4,256]{1,0:T(4,128)S(1)}, bf16[512,3584]{1,0:T(8,128)(2,1)}, bf16[512,1792]{1,0:T(8,128)(2,1)S(1)}, bf16[512,5376]{1,0:T(8,128)(2,1)}) conditional(s32[]{:T(128)} %convert_element_type.4, (s32[2,256]{1,0:T(2,128)}, bf16[256,3584]{1,0:T(8,128)(2,1)}) %tuple.37, (s32[2,256]{1,0:T(2,128)}, bf16[256,3584]{1,0:T(8,128)(2,1)}) %tuple.38), branch_computations={%region_0.0_spmd, %region_1.0_spmd} | conditional | bytes 7340064 | solution.py:384
  1.4 6.1 %dispatch_rows.2 = (s32[4,256]{1,0:T(4,128)S(1)}, bf16[512,5376]{1,0:T(8,128)(2,1)}) custom-call(s32[2,256]{1,0:T(2,128)} %get-tuple-element.50.ids_ref, bf16[256,3584]{1,0:T(8,128)(2,1)} %get-tuple-element.51.tok_ref), custom_call_target="tpu_custom_call" | custom-call | tf_op jit(solution)/shard_map/cond/branch_0_fun/dispatch_rows/pallas_call | solution.py:68
  7.6 8.1 %collective-permute-done = bf16[1,3584,1280]{2,1,0:T(8,128)(2,1)} collective-permute-done((bf16[1,3584,1280]{2,1,0:T(8,128)(2,1)}, bf16[1,3584,1280]{2,1,0:T(8,128)(2,1)}, u32[]{:S(2)}, u32[]{:S(2)}) %collective-permute-start) | collective-permute-done | bytes 9175072 | tf_op jit(solution)/shard_map/ppermute | solution.py:357
  15.7 13.1 %collective-permute-done.1 = bf16[1,1280,3584]{2,1,0:T(8,128)(2,1)} collective-permute-done((bf16[1,1280,3584]{2,1,0:T(8,128)(2,1)}, bf16[1,1280,3584]{2,1,0:T(8,128)(2,1)}, u32[]{:S(2)}, u32[]{:S(2)}) %collective-permute-start.1) | collective-permute-done | bytes 9175072 | tf_op jit(solution)/shard_map/ppermute | solution.py:358
  28.8 0.0 copy-done.4
  28.8 145.6 %conditional.3 = (bf16[256,3584]{1,0:T(8,128)(2,1)S(1)}) conditional(s32[]{:T(128)} %convert_element_type.4, (bf16[512,5376]{1,0:T(8,128)(2,1)}, bf16[3584,1280]{1,0:T(8,128)(2,1)}, bf16[3584,1280]{1,0:T(8,128)(2,1)}, bf16[1280,3584]{1,0:T(8,128)(2,1)}, bf16[1280,3584]{1,0:T(8,128)(2,1)}, /*index=5*/s32[4,256]{1,0:T(4,128)S(1)}, ...), branch_computations={%region_2.0_spmd, %region_3.0_spmd} | conditional | flops 30064771072 | bytes 144965696 | solution.py:387
  28.8 48.7 %all_to_all.21 = bf16[64,8,5376]{2,1,0:T(8,128)(2,1)} all-to-all(bf16[64,8,5376]{2,1,0:T(8,128)(2,1)} %bitcast.20), channel_id=1, replica_groups=mesh['dp'=2,'expert'=64] {'expert'}, dimensions={0} | all-to-all | bytes 11010048 | tf_op jit(solution)/shard_map/cond/branch_0_fun/all_to_all | solution.py:350
  77.5 37.4 %expert_both.1.after = bf16[512,5376]{1,0:T(8,128)(2,1)} custom-call(bf16[512,5376]{1,0:T(8,128)(2,1)} %bitcast.28, bf16[3584,1280]{1,0:T(8,128)(2,1)} %get-tuple-element.62.ia, bf16[3584,1280]{1,0:T(8,128)(2,1)} %get-tuple-element.63.ib, bf16[1280,3584]{1,0:T(8,128)(2,1)} %get-tuple-element.64.oa, bf16[1280,3584]{1,0:T(8,128)(2,1)} %get-tuple-element.65.ob), custom_call_target="tpu_custom_call" | custom-call | flops 28185722880 | bytes 47710208 | tf_op jit(solution)/shard_map/cond/branch_0_fun/expert_both/pallas_call | solution.py:309
  114.9 0.0 copy-start.2
  114.9 6.0 %all-to-all-start.2 = ((bf16[64,8,5376]{2,1,0:T(8,128)(2,1)}), bf16[64,8,5376]{2,1,0:T(8,128)(2,1)}, u32[]{:S(2)}, u32[]{:S(2)}) async-start(bf16[64,8,5376]{2,1,0:T(8,128)(2,1)} %bitcast.18), calls=%async_computation.2 | async-start | bytes 11010048 | tf_op jit(solution)/shard_map/cond/branch_0_fun/all_to_all | solution.py:350
  120.9 0.0 copy-start.1
  120.9 2.6 %copy-done.1 = bf16[512,5376]{1,0:T(8,128)(2,1)S(1)} copy-done((bf16[512,5376]{1,0:T(8,128)(2,1)S(1)}, bf16[512,5376]{1,0:T(8,128)(2,1)}, u32[]{:S(2)}) %copy-start.1) | copy-done | bytes 5505048 | tf_op jit(solution)/shard_map/cond
  123.5 0.3 gate_matrices.1.weight_ref
  123.8 45.6 %all-to-all-done.2 = bf16[64,8,5376]{2,1,0:T(8,128)(2,1)} async-done(((bf16[64,8,5376]{2,1,0:T(8,128)(2,1)}), bf16[64,8,5376]{2,1,0:T(8,128)(2,1)}, u32[]{:S(2)}, u32[]{:S(2)}) %all-to-all-start.2) | async-done | bytes 5505056 | tf_op jit(solution)/shard_map/cond/branch_0_fun/all_to_all | solution.py:350
  169.4 0.0 copy-done.2
  169.4 4.7 %weighted_rows.1 = bf16[256,3584]{1,0:T(8,128)(2,1)S(1)} custom-call(bf16[3,512,256]{2,1,0:T(8,128)(2,1)S(1)} %gate_matrices.1.weight_ref, bf16[256,3584]{1,0:T(8,128)(2,1)S(1)} %copy-done.2, bf16[512,5376]{1,0:T(8,128)(2,1)} %bitcast.5.back_ref.pack_ref, bf16[512,5376]{1,0:T(8,128)(2,1)} %bitcast.5.back_ref.pack_ref), custom_call_target="tpu_custom_call" | custom-call | tf_op jit(solution)/shard_map/cond/branch_0_fun/weighted_rows/pallas_call | solution.py:119
  174.4 0.0 copy-start.3
  174.4 1.2 copy-done.3
  (2 shorter events, 0.0 us)
Async XLA Ops:
  0.0 15.7 %collective-permute-start = (bf16[1,3584,1280]{2,1,0:T(8,128)(2,1)}, bf16[1,3584,1280]{2,1,0:T(8,128)(2,1)}, u32[]{:S(2)}, u32[]{:S(2)}) collective-permute-start(bf16[1,3584,1280]{2,1,0:T(8,128)(2,1)} %param.12), channel_id=1, source_target_pairs={{0,64},{64,0},{1,65},{65,1},{2,66},{66,2},{3,67},{67,3},{4,68},{68... | collective-permute-start | bytes 27525128 | tf_op jit(solution)/shard_map/ppermute | solution.py:357
  1.4 27.4 %collective-permute-start.1 = (bf16[1,1280,3584]{2,1,0:T(8,128)(2,1)}, bf16[1,1280,3584]{2,1,0:T(8,128)(2,1)}, u32[]{:S(2)}, u32[]{:S(2)}) collective-permute-start(bf16[1,1280,3584]{2,1,0:T(8,128)(2,1)} %param.13), channel_id=1, source_target_pairs={{0,64},{64,0},{1,65},{65,1},{2,66},{66,2},{3,67},{67,3},{4,68},{68... | collective-permute-start | bytes 27525128 | tf_op jit(solution)/shard_map/ppermute | solution.py:358
  1.4 27.4 %copy-start.4 = (f32[256,2]{0,1:T(2,128)S(1)}, f32[256,2]{0,1:T(2,128)}, u32[]{:S(2)}) copy-start(f32[256,2]{0,1:T(2,128)} %param.11) | copy-start | bytes 6148
  114.9 54.5 %copy-start.2 = (bf16[256,3584]{1,0:T(8,128)(2,1)S(1)}, bf16[256,3584]{1,0:T(8,128)(2,1)}, u32[]{:S(2)}) copy-start(bf16[256,3584]{1,0:T(8,128)(2,1)} %get-tuple-element.66.tok_ref) | copy-start | bytes 5505028 | tf_op jit(solution)/shard_map/cond
  114.9 54.5 %all-to-all-start.2 = ((bf16[64,8,5376]{2,1,0:T(8,128)(2,1)}), bf16[64,8,5376]{2,1,0:T(8,128)(2,1)}, u32[]{:S(2)}, u32[]{:S(2)}) async-start(bf16[64,8,5376]{2,1,0:T(8,128)(2,1)} %bitcast.18), calls=%async_computation.2 | async-start | bytes 11010048 | tf_op jit(solution)/shard_map/cond/branch_0_fun/all_to_all | solution.py:350
  120.9 2.6 %copy-start.1 = (bf16[512,5376]{1,0:T(8,128)(2,1)S(1)}, bf16[512,5376]{1,0:T(8,128)(2,1)}, u32[]{:S(2)}) copy-start(bf16[512,5376]{1,0:T(8,128)(2,1)} %expert_both.1.after) | copy-start | bytes 16515076 | tf_op jit(solution)/shard_map/cond
  174.4 1.2 copy-start.3
